TPU v7x, 512 devices: a whole 4x4x16 slice. The times are simulated.
512 devices in a mesh: rows: 64 (over x, z), grp: 8 (over y, core).
Axes of the slice: x: 4, y: 4, z: 16, core: 2. Of those that a mesh axis runs over, the one named last changes fastest.
Arguments:
- activations: bfloat16 [131072, 8192], P(('rows', 'grp')), may hold values from -120 to 120
- start_basis: bfloat16 [131072, 64], P(('rows', 'grp')), may hold values from -6 to 6
Outputs:
- new_basis: float32 [131072, 64], P(('rows', 'grp'))
- rfactor: float32 [64, 64], replicated
All inputs are finite; a program needn't handle non-finite values.
Results may differ from a plain program's by a relative error of at most 0.0029.
Values may be sent and summed in bfloat16 or wider, within the bound.
A program may use at most 64 MiB of HBM per device.

v0:
```python
import jax
import jax.numpy as jnp
from jax import lax
from jax.sharding import PartitionSpec as P


def on_device(activations, start_basis):
    devices_all = lax.axis_size("rows") * lax.axis_size("grp")
    total_rows = activations.shape[0] * devices_all
    width = activations.shape[1]
    scaling = 1.0 / jnp.sqrt(jnp.float32(total_rows))
    partial_proj = (
        jnp.einsum("rd,rk->dk", activations, start_basis, preferred_element_type=jnp.float32)
        * scaling
    )
    projected = lax.psum(partial_proj, ("rows", "grp")).astype(jnp.bfloat16)
    image = jnp.dot(activations, projected, preferred_element_type=jnp.float32)
    image = image / jnp.sqrt(jnp.float32(width))
    gram_local = jnp.dot(image.T, image, precision=lax.Precision.HIGHEST) / jnp.float32(total_rows)
    gram_total = lax.psum(gram_local, ("rows", "grp"))
    lower = jnp.linalg.cholesky(gram_total)
    new_basis = jax.scipy.linalg.solve_triangular(lower, image.T, lower=True).T
    return (new_basis, lower.T)


def solution(mesh):
    in_specs = (P(("rows", "grp"), None), P(("rows", "grp"), None))
    out_specs = (P(("rows", "grp"), None), P())
    return jax.shard_map(
        on_device, mesh=mesh, in_specs=in_specs, out_specs=out_specs, check_vma=False
    )
```

profile of v0, /device:TPU:1, one launch (start us, length us, event | category | flops | bytes accessed | tf_op | source)
XLA Modules:
  0.0 242.1 jit_solution(3484856757910436634)
XLA Ops:
  0.6 0.0 copy-start
  0.6 0.7 copy-done
  1.4 3.0 %convolution_multiply_fusion = f32[8192,64]{0,1:T(8,128)S(1)} fusion(bf16[256,64]{0,1:T(8,128)(2,1)S(1)} %copy-done, bf16[256,8192]{1,0:T(8,128)(2,1)} %param.2), kind=kOutput, calls=%fused_computation | convolution fusion | flops 268959744 | bytes 6324224 | tf_op jit(solution)/shard_map/rd,rk->dk/dot_general | solution.py:13
  4.4 119.7 %all-reduce.1 = bf16[8192,64]{0,1:T(8,128)(2,1)S(1)} all-reduce(f32[8192,64]{0,1:T(8,128)S(1)} %convolution_multiply_fusion), channel_id=1, replica_groups=mesh['rows'=64,'grp'=8] {'rows','grp'}, use_global_device_ids=true, to_apply=%region_0.0 | all-reduce | flops 524288 | bytes 3145728 | tf_op jit(solution)/shard_map/psum | solution.py:16
  124.1 3.6 %convolution_multiply_fusion.1 = f32[64,256]{1,0:T(8,128)S(1)} fusion(bf16[256,8192]{1,0:T(8,128)(2,1)} %param.2, bf16[8192,64]{0,1:T(8,128)(2,1)S(1)} %all-reduce.1), kind=kOutput, calls=%fused_computation.1 | convolution fusion | flops 268451840 | bytes 5308416 | tf_op jit(solution)/shard_map/dot_general | solution.py:17
  127.7 0.2 convolution_multiply_fusion.2
  127.9 100.4 %psum.15 = f32[64,64]{0,1:T(8,128)S(1)} all-reduce(f32[64,64]{0,1:T(8,128)S(1)} %convolution_multiply_fusion.2), channel_id=1, replica_groups=mesh['rows'=64,'grp'=8] {'rows','grp'}, use_global_device_ids=true, to_apply=%region_1.0 | all-reduce | flops 4096 | bytes 32768 | tf_op jit(solution)/shard_map/psum | solution.py:20
  228.3 0.1 copy.8
  228.4 5.8 %cholesky.16 = f32[64,64]{1,0:T(8,128)S(1)} custom-call(f32[64,64]{1,0:T(8,128)S(1)} %fusion.3), custom_call_target="Cholesky" | custom-call | tf_op jit(solution)/shard_map/jit(cholesky)/cholesky | solution.py:21
  234.3 0.6 compare_reduce_fusion
  234.9 0.7 fusion.4
  235.6 0.7 copy.9
  236.3 4.9 %custom-call.7 = f32[1,64,64]{1,2,0:T(8,128)S(1)} custom-call(f32[1,64,64]{2,1,0:T(8,128)S(1)} %get-tuple-element.7), custom_call_target="InvertDiagBlocksLowerTriangular" | custom-call | tf_op jit(solution)/shard_map/jit(_solve_triangular)/triangular_solve | solution.py:22
  241.2 0.9 fusion.1
  (2 shorter events, 0.0 us)
Async XLA Ops:
  0.6 0.8 copy-start
where the time goes:
time: 242 us
  blocking collectives  220 us (91%)
  other arithmetic  12.1 us (5%)
  matrix products  7.73 us (3%)
    psum x1, blocking collectives, on_device(): projected = lax.psum(partial_proj, ('rows', 'grp')).astype(jnp.bfloat16)  120 us
    psum x1, blocking collectives, on_device(): gram_total = lax.psum(gram_local, ('rows', 'grp'))  100 us
    another operation x3, other arithmetic, on_device(): lower = jnp.linalg.cholesky(gram_total)  6.52 us
    another operation x1, other arithmetic, on_device(): new_basis = jax.scipy.linalg.solve_triangular(lower, image.T, lower=True).T  4.89 us

commit v1 on v0

v1 whole, which is shorter than its diff:
```python
import functools
import math

import jax
import jax.numpy as jnp
from jax import lax
from jax.experimental import pallas as pl
from jax.experimental.pallas import tpu as pltpu
from jax.sharding import PartitionSpec as P

MESH = pl.DeviceIdType.MESH
F32 = jnp.float32
BF16 = jnp.bfloat16
ROWS, D, K = 256, 8192, 64
TOTAL = 131072
CHUNK = 512


def comm_kernel(a_hbm, s_hbm, img_ref, gram_ref, a_v, s_v, other, land_c, r1, land_1, r2, land_2, r3, land_z, pall,
                g_own, land_g, g_z, g_all,
                load_sem, c_send, c_recv, s1_send, s1_recv, s2_send, s2_recv, z_send, z_recv,
                zg_send, zg_recv, xy_send, xy_recv, f_send, f_recv,
                g1_send, g1_recv, g2_send, g2_recv, g3_send, g3_recv):
    r = lax.axis_index("rows")
    g = lax.axis_index("grp")
    x, z = r // 16, r % 16
    y, c = g // 2, g % 2

    def dev(xx, yy, zz, cc):
        return (xx * 16 + zz, yy * 2 + cc)

    partner = dev(x, y, z, 1 - c)

    def plane(k):
        return (x + k // 8) % 4, (y + (k // 2) % 4) % 4, (c + k % 2) % 2

    def remote(src, dst, ss, rs, target):
        return pltpu.make_async_remote_copy(src_ref=src, dst_ref=dst, send_sem=ss, recv_sem=rs, device_id=target,
                                            device_id_type=MESH)

    pltpu.make_async_copy(s_hbm, s_v, load_sem.at[16]).start()
    order = []
    for half in (1, 0):
        for j in range(8):
            order.append((half, j))
    for half, j in order:
        ch = (c if half == 0 else 1 - c) * 8 + j
        pltpu.make_async_copy(a_hbm.at[:, pl.ds(pl.multiple_of(ch * CHUNK, CHUNK), CHUNK)], a_v.at[ch], load_sem.at[ch]).start()

    bar = pltpu.get_barrier_semaphore()

    @pl.loop(1, 32)
    def _(k):
        xx, yy, cc = plane(k)
        pl.semaphore_signal(bar, inc=1, device_id=dev(xx, yy, z, cc), device_id_type=MESH)

    @pl.loop(1, 16)
    def _(k):
        pl.semaphore_signal(bar, inc=1, device_id=dev(x, y, (z + k) % 16, c), device_id_type=MESH)

    pltpu.make_async_copy(s_hbm, s_v, load_sem.at[16]).wait()
    st = s_v[...].astype(F32).T.astype(BF16)

    def partial(ch, j, dst):
        pltpu.make_async_copy(a_hbm.at[:, pl.ds(0, CHUNK)], a_v.at[ch], load_sem.at[ch]).wait()
        part = jnp.dot(st, a_v[ch], preferred_element_type=F32)
        q, a = j // 4, j % 4
        for s in range(4):
            for b in range(4):
                dst[q * 4 + s, a, b] = part[16 * s:16 * s + 16, 128 * b:128 * b + 128]

    @pl.loop(0, 8)
    def _(j):
        partial((1 - c) * 8 + j, j, other)

    pl.semaphore_wait(bar, 46)

    c_copies = [remote(other.at[i], land_c.at[i], c_send.at[i], c_recv.at[i], partner) for i in range(8)]
    for cp in c_copies:
        cp.start()

    @pl.loop(0, 8)
    def _(j):
        partial(c * 8 + j, j, r1)

    me_a = (x, y)
    me_b = (y, x)

    def first_peer(q, k):
        return dev((x + k) % 4, y, z, c) if q == 0 else dev(x, (y + k) % 4, z, c)

    def second_peer(q, k):
        return first_peer(1 - q, k)

    copies_1 = {}
    for s in range(4):
        for q in range(2):
            i = q * 4 + s
            c_copies[i].wait_recv()
            r1[i] = r1[i] + land_c[i]
            for k in (1, 2, 3):
                n = i * 3 + k - 1
                cp = remote(r1.at[i, (me_a[q] + k) % 4], land_1.at[i, k - 1], s1_send.at[n], s1_recv.at[n], first_peer(q, k))
                cp.start()
                copies_1[i, k] = cp
    copies_2 = {}
    for s in range(4):
        for q in range(2):
            i = q * 4 + s
            for k in (1, 2, 3):
                copies_1[i, k].wait_recv()
            r2[i] = (r1[i, me_a[q]] + land_1[i, 0]) + (land_1[i, 1] + land_1[i, 2])
            for k in (1, 2, 3):
                n = i * 3 + k - 1
                cp = remote(r2.at[i, (me_b[q] + k) % 4], land_2.at[i, k - 1], s2_send.at[n], s2_recv.at[n], second_peer(q, k))
                cp.start()
                copies_2[i, k] = cp

    def z_copy(i, slot):
        zo = 4 * (i % 4) + 2 * (i // 4) + c
        return zo, remote(r3.at[i], land_z.at[slot], z_send.at[i], z_recv.at[slot], dev(x, y, zo, c))

    for s in range(4):
        for q in range(2):
            i = q * 4 + s
            for k in (1, 2, 3):
                copies_2[i, k].wait_recv()
            r3[i] = (r2[i, me_b[q]] + land_2[i, 0]) + (land_2[i, 1] + land_2[i, 2])
            zo = 4 * s + 2 * q + c

            @pl.when(zo != z)
            def _(i=i, zo=zo):
                z_copy(i, (zo - z + 16) % 16)[1].start()

    my_s, my_q = z // 4, (z % 4) // 2
    my_i = my_q * 4 + my_s
    owner = z % 2 == c

    def place(q):
        return (c * 2 + q) * 16 + jnp.where(q == 0, x * 4 + y, y * 4 + x)

    def zg_copy(k):
        here = pall.at[place(my_q), my_s]
        return remote(here, here, zg_send.at[k], zg_recv.at[my_i], dev(x, y, (z + k) % 16, c))

    @pl.when(owner)
    def _():
        total = r3[my_i]
        for k in range(1, 16):
            pltpu.make_async_copy(land_z.at[k], land_z.at[k], z_recv.at[k]).wait()
        for k in range(1, 16):
            total = total + land_z[k]
        pall[place(my_q), my_s] = (total * (1.0 / math.sqrt(TOTAL))).astype(BF16)

        @pl.loop(1, 16)
        def _(k):
            zg_copy(k).start()

    def xy_copy(k, q, s):
        here = pall.at[place(q), s]
        return remote(here, here, xy_send.at[k, q], xy_recv.at[k, q], dev((x + k // 4) % 4, (y + k % 4) % 4, z, c))

    for j in range(8):
        off = jnp.where(owner, (0, 2, 14, 4, 12, 6, 10, 8)[j], (1, 15, 3, 13, 5, 11, 7, 9)[j])
        zz = (z + off) % 16
        s, q = zz // 4, (zz % 4) // 2

        @pl.when(off != 0)
        def _(s=s, q=q):
            here = pall.at[place(q), s]
            pltpu.make_async_copy(here, here, zg_recv.at[q * 4 + s]).wait()

        @pl.loop(1, 16)
        def _(k, q=q, s=s):
            xy_copy(k, q, s).start()

    def forward(k, q):
        xx, yy = (x - k // 4 + 4) % 4, (y - k % 4 + 4) % 4
        p = (c * 2 + q) * 16 + (xx * 4 + yy if q == 0 else yy * 4 + xx)
        return p, remote(pall.at[p], pall.at[p], f_send, f_recv, partner)

    for q in range(2):
        forward(0, q)[1].start()

    @pl.loop(1, 16)
    def _(k):
        for q in range(2):
            p, cp = forward(k, q)
            pltpu.make_async_copy(pall.at[p], pall.at[p], xy_recv.at[k, q]).wait()
            cp.start()

    def image_part(half, acc):
        def body(j, acc):
            ch = half * 8 + j
            pt = jnp.concatenate([pall[ch * 4 + b].reshape(64, 128) for b in range(4)], axis=1)
            return acc + lax.dot_general(a_v[ch], pt, (((1,), (1,)), ((), ())), preferred_element_type=F32)
        return lax.fori_loop(0, 8, body, acc)

    acc = image_part(c, jnp.zeros((ROWS, K), F32))
    theirs = pall.at[pl.ds((1 - c) * 32, 32)]
    pltpu.make_async_copy(theirs, theirs, f_recv).wait()
    acc = image_part(1 - c, acc)
    img = acc * (1.0 / math.sqrt(D))
    img_ref[...] = img
    gram = lax.dot_general(img, img, (((0,), (0,)), ((), ())), precision=lax.Precision.HIGHEST, preferred_element_type=F32)
    gram = gram * (1.0 / TOTAL)

    for m in range(32):
        g_own[m] = gram[2 * m:2 * m + 2, :]
    me = (x * 4 + y) * 2 + c

    def g1_copy(k):
        xx, yy, cc = plane(k)
        return remote(g_own.at[(xx * 4 + yy) * 2 + cc], land_g.at[k], g1_send.at[k], g1_recv.at[k], dev(xx, yy, z, cc))

    @pl.loop(1, 32)
    def _(k):
        g1_copy(k).start()

    tot = g_own[me]
    for k in range(1, 32):
        g1_copy(k).wait_recv()
    for k in range(1, 32):
        tot = tot + land_g[k]
    g_z[z] = tot

    def g2_copy(k, zs):
        return remote(g_z.at[zs], g_z.at[zs], g2_send.at[k], g2_recv.at[zs], dev(x, y, (z + k) % 16, c))

    @pl.loop(1, 16)
    def _(k):
        g2_copy(k, z).start()

    @pl.loop(1, 16)
    def _(k):
        g2_copy(k, (z + k) % 16).wait_recv()

    tot = g_z[0]
    for k in range(1, 16):
        tot = tot + g_z[k]
    g_all[me] = tot

    def g3_copy(k):
        xx, yy, cc = plane(k)
        return remote(g_all.at[me], g_all.at[me], g3_send.at[k], g3_recv.at[me], dev(xx, yy, z, cc))

    @pl.loop(1, 32)
    def _(k):
        g3_copy(k).start()

    @pl.loop(1, 32)
    def _(k):
        xx, yy, cc = plane(k)
        m = (xx * 4 + yy) * 2 + cc
        pltpu.make_async_copy(g_all.at[m], g_all.at[m], g3_recv.at[m]).wait()

    gram_ref[...] = g_all[...]

    for cp in c_copies:
        cp.wait_send()
    for i in range(8):
        for k in (1, 2, 3):
            copies_1[i, k].wait_send()
            copies_2[i, k].wait_send()
    for i in range(8):
        @pl.when(4 * (i % 4) + 2 * (i // 4) + c != z)
        def _(i=i):
            z_copy(i, 1)[1].wait_send()

    @pl.when(owner)
    def _():
        @pl.loop(1, 16)
        def _(k):
            zg_copy(k).wait_send()

    @pl.loop(1, 16)
    def _(k):
        for q in range(2):
            pltpu.make_async_copy(pall.at[q], pall.at[q], xy_send.at[k, q]).wait()
        g2_copy(k, z).wait_send()

    pltpu.make_async_copy(theirs, theirs, f_send).wait()

    @pl.loop(1, 32)
    def _(k):
        g1_copy(k).wait_send()
        g3_copy(k).wait_send()


def comm(activations, start_basis):
    dma = pltpu.SemaphoreType.DMA
    return pl.pallas_call(
        comm_kernel,
        out_shape=(jax.ShapeDtypeStruct((ROWS, K), F32), jax.ShapeDtypeStruct((32, 2, K), F32)),
        in_specs=[pl.BlockSpec(memory_space=pl.ANY)] * 2,
        out_specs=(pl.BlockSpec(memory_space=pltpu.VMEM),) * 2,
        scratch_shapes=[
            pltpu.VMEM((16, ROWS, CHUNK), BF16),
            pltpu.VMEM((ROWS, K), BF16),
            pltpu.VMEM((8, 4, 4, 16, 128), F32),
            pltpu.VMEM((8, 4, 4, 16, 128), F32),
            pltpu.VMEM((8, 4, 4, 16, 128), F32),
            pltpu.VMEM((8, 3, 4, 16, 128), F32),
            pltpu.VMEM((8, 4, 16, 128), F32),
            pltpu.VMEM((8, 3, 16, 128), F32),
            pltpu.VMEM((8, 16, 128), F32),
            pltpu.VMEM((16, 16, 128), F32),
            pltpu.VMEM((64, 4, 16, 128), BF16),
            pltpu.VMEM((32, 2, K), F32),
            pltpu.VMEM((32, 2, K), F32),
            pltpu.VMEM((16, 2, K), F32),
            pltpu.VMEM((32, 2, K), F32),
            dma((17,)), dma((8,)), dma((8,)), dma((24,)), dma((24,)), dma((24,)), dma((24,)), dma((8,)), dma((16,)),
            dma((16,)), dma((8,)), dma((16, 2)), dma((16, 2)), dma, dma,
            dma((32,)), dma((32,)), dma((16,)), dma((16,)), dma((32,)), dma((32,)),
        ],
        compiler_params=pltpu.CompilerParams(collective_id=0, has_side_effects=True, vmem_limit_bytes=40 << 20),
        cost_estimate=pl.CostEstimate(flops=4 * ROWS * D * K, bytes_accessed=ROWS * D * 2, transcendentals=0),
        name="reduce_project_gram",
    )(activations, start_basis)


def on_device(activations, start_basis):
    image, gram = comm(activations, start_basis)
    lower = jnp.linalg.cholesky(gram.reshape(K, K))
    new_basis = jax.scipy.linalg.solve_triangular(lower, image.T, lower=True).T
    return (new_basis, lower.T)


def solution(mesh):
    in_specs = (P(("rows", "grp"), None), P(("rows", "grp"), None))
    out_specs = (P(("rows", "grp"), None), P())
    return jax.shard_map(
        on_device, mesh=mesh, in_specs=in_specs, out_specs=out_specs, check_vma=False
    )
```

time: 242 us -> 94 us (0.39)
  blocking collectives: 220 us -> 0 us
  Pallas kernels: 0 us -> 76.2 us
  matrix products: 7.73 us -> 0.95 us
    psum x2 -> x0, blocking collectives: 220 us -> none  [the longest x1 120 us: on_device(): projected = lax.psum(partial_proj, ('rows', 'grp')).astype(jnp.bfloat16)]
    pallas_call x0 -> x1, Pallas kernels: none -> 76.2 us  [comm(): pl.pallas_call(comm_kernel, out_shape=(jax.ShapeDtypeStruct((ROWS, K), F3...]
    dot_general x3 -> x0, matrix products: 6.83 us -> none  [the longest x1 3.58 us: on_device(): image = jnp.dot(activations, projected, preferred_element_type=jnp.float32)]
where the time goes in v1:
time: 94 us; the launch traced here: 93.8 us
  Pallas kernels  76.2 us (81%)
  other arithmetic  12.1 us (13%)
  local copies, waits for them, and re-layouts  3.83 us (4%)
  matrix products  0.95 us (1%)
    pallas_call x1, Pallas kernels, comm(): pl.pallas_call(comm_kernel, out_shape=(jax.ShapeDtypeStruct((ROWS, K), F3...  76.2 us
    another operation x3, other arithmetic, on_device(): lower = jnp.linalg.cholesky(gram.reshape(K, K))  6.52 us
    another operation x1, other arithmetic, on_device(): new_basis = jax.scipy.linalg.solve_triangular(lower, image.T, lower=True).T  4.89 us
    unnamed x4, local copies, waits for them, and re-layouts  3.76 us

profile of v1, /device:TPU:1, one launch (start us, length us, event | category | flops | bytes accessed | tf_op | source)
XLA Modules:
  0.0 93.8 jit_solution(476934704882961518)
XLA Ops:
  0.6 0.9 copy.8.s_hbm
  1.5 0.0 copy-start
  1.5 2.2 %copy-done = bf16[256,8192]{1,0:T(8,128)(2,1)S(1)} copy-done((bf16[256,8192]{1,0:T(8,128)(2,1)S(1)}, bf16[256,8192]{1,0:T(8,128)(2,1)}, u32[]{:S(2)}) %copy-start) | copy-done | bytes 4194328
  3.7 76.2 %reduce_project_gram.1 = (f32[256,64]{1,0:T(8,128)S(1)}, f32[32,2,64]{2,1,0:T(2,128)S(1)}) custom-call(bf16[256,8192]{1,0:T(8,128)(2,1)S(1)} %copy-done, bf16[256,64]{1,0:T(8,128)(2,1)S(1)} %copy.8.s_hbm), custom_call_target="tpu_custom_call" | custom-call | flops 536870912 | bytes 4194304 | tf_op jit(solution)/shard_map/reduce_project_gram/pallas_call | solution.py:292
  79.9 0.1 copy.9
  80.0 5.8 %cholesky.16 = f32[64,64]{1,0:T(8,128)S(1)} custom-call(f32[64,64]{1,0:T(8,128)S(1)} %fusion.2), custom_call_target="Cholesky" | custom-call | tf_op jit(solution)/shard_map/jit(cholesky)/cholesky | solution.py:325
  85.9 0.6 compare_reduce_fusion
  86.5 0.7 fusion.3
  87.2 0.7 copy.10
  87.9 4.9 %custom-call.7 = f32[1,64,64]{1,2,0:T(8,128)S(1)} custom-call(f32[1,64,64]{2,1,0:T(8,128)S(1)} %get-tuple-element.11), custom_call_target="InvertDiagBlocksLowerTriangular" | custom-call | tf_op jit(solution)/shard_map/jit(_solve_triangular)/triangular_solve | solution.py:326
  92.8 0.9 %fusion = f32[256,64]{0,1:T(8,128)} fusion(f32[256,64]{1,0:T(8,128)S(1)} %get-tuple-element.4, f32[1,64,64]{1,2,0:T(8,128)S(1)} %custom-call.7), kind=kOutput, calls=%fused_computation | convolution fusion | flops 12582912 | bytes 147456 | tf_op jit(solution)/shard_map/jit(_solve_triangular)/triangular_solve | solution.py:326
  (2 shorter events, 0.0 us)
Async XLA Ops:
  1.5 2.2 %copy-start = (bf16[256,8192]{1,0:T(8,128)(2,1)S(1)}, bf16[256,8192]{1,0:T(8,128)(2,1)}, u32[]{:S(2)}) copy-start(bf16[256,8192]{1,0:T(8,128)(2,1)} %a_hbm.1) | copy-start | bytes 12582916

commit v2 on v1

--- a/solution.py
+++ b/solution.py
@@ -38,6 +38,17 @@
         return pltpu.make_async_remote_copy(src_ref=src, dst_ref=dst, send_sem=ss, recv_sem=rs, device_id=target,
                                             device_id_type=MESH)
 
+    bar = pltpu.get_barrier_semaphore()
+
+    @pl.loop(1, 16)
+    def _(k):
+        pl.semaphore_signal(bar, inc=1, device_id=dev(x, y, (z + 8 + k // 2 * (1 - k % 2 * 2) + 16) % 16, c), device_id_type=MESH)
+
+    @pl.loop(1, 32)
+    def _(k):
+        xx, yy, cc = plane(k)
+        pl.semaphore_signal(bar, inc=1, device_id=dev(xx, yy, z, cc), device_id_type=MESH)
+
     pltpu.make_async_copy(s_hbm, s_v, load_sem.at[16]).start()
     order = []
     for half in (1, 0):
@@ -47,19 +58,8 @@
         ch = (c if half == 0 else 1 - c) * 8 + j
         pltpu.make_async_copy(a_hbm.at[:, pl.ds(pl.multiple_of(ch * CHUNK, CHUNK), CHUNK)], a_v.at[ch], load_sem.at[ch]).start()
 
-    bar = pltpu.get_barrier_semaphore()
-
-    @pl.loop(1, 32)
-    def _(k):
-        xx, yy, cc = plane(k)
-        pl.semaphore_signal(bar, inc=1, device_id=dev(xx, yy, z, cc), device_id_type=MESH)
-
-    @pl.loop(1, 16)
-    def _(k):
-        pl.semaphore_signal(bar, inc=1, device_id=dev(x, y, (z + k) % 16, c), device_id_type=MESH)
-
     pltpu.make_async_copy(s_hbm, s_v, load_sem.at[16]).wait()
-    st = s_v[...].astype(F32).T.astype(BF16)
+    st = s_v[...]
 
     def partial(ch, j, dst):
         pltpu.make_async_copy(a_hbm.at[:, pl.ds(0, CHUNK)], a_v.at[ch], load_sem.at[ch]).wait()
@@ -193,16 +193,16 @@
         def body(j, acc):
             ch = half * 8 + j
             pt = jnp.concatenate([pall[ch * 4 + b].reshape(64, 128) for b in range(4)], axis=1)
-            return acc + lax.dot_general(a_v[ch], pt, (((1,), (1,)), ((), ())), preferred_element_type=F32)
+            return acc + lax.dot_general(pt, a_v[ch], (((1,), (1,)), ((), ())), preferred_element_type=F32)
         return lax.fori_loop(0, 8, body, acc)
 
-    acc = image_part(c, jnp.zeros((ROWS, K), F32))
+    acc = image_part(c, jnp.zeros((K, ROWS), F32))
     theirs = pall.at[pl.ds((1 - c) * 32, 32)]
     pltpu.make_async_copy(theirs, theirs, f_recv).wait()
     acc = image_part(1 - c, acc)
     img = acc * (1.0 / math.sqrt(D))
     img_ref[...] = img
-    gram = lax.dot_general(img, img, (((0,), (0,)), ((), ())), precision=lax.Precision.HIGHEST, preferred_element_type=F32)
+    gram = lax.dot_general(img, img, (((1,), (1,)), ((), ())), precision=lax.Precision.HIGHEST, preferred_element_type=F32)
     gram = gram * (1.0 / TOTAL)
 
     for m in range(32):
@@ -291,12 +291,12 @@
     dma = pltpu.SemaphoreType.DMA
     return pl.pallas_call(
         comm_kernel,
-        out_shape=(jax.ShapeDtypeStruct((ROWS, K), F32), jax.ShapeDtypeStruct((32, 2, K), F32)),
+        out_shape=(jax.ShapeDtypeStruct((K, ROWS), F32), jax.ShapeDtypeStruct((32, 2, K), F32)),
         in_specs=[pl.BlockSpec(memory_space=pl.ANY)] * 2,
         out_specs=(pl.BlockSpec(memory_space=pltpu.VMEM),) * 2,
         scratch_shapes=[
             pltpu.VMEM((16, ROWS, CHUNK), BF16),
-            pltpu.VMEM((ROWS, K), BF16),
+            pltpu.VMEM((K, ROWS), BF16),
             pltpu.VMEM((8, 4, 4, 16, 128), F32),
             pltpu.VMEM((8, 4, 4, 16, 128), F32),
             pltpu.VMEM((8, 4, 4, 16, 128), F32),
@@ -314,17 +314,55 @@
             dma((16,)), dma((8,)), dma((16, 2)), dma((16, 2)), dma, dma,
             dma((32,)), dma((32,)), dma((16,)), dma((16,)), dma((32,)), dma((32,)),
         ],
-        compiler_params=pltpu.CompilerParams(collective_id=0, has_side_effects=True, vmem_limit_bytes=40 << 20),
+        compiler_params=pltpu.CompilerParams(collective_id=0, has_side_effects=True, vmem_limit_bytes=60 << 20),
         cost_estimate=pl.CostEstimate(flops=4 * ROWS * D * K, bytes_accessed=ROWS * D * 2, transcendentals=0),
         name="reduce_project_gram",
     )(activations, start_basis)
 
 
+def factor_kernel(gram_ref, img_ref, basis_ref, r_ref):
+    g = [gram_ref[8 * i:8 * i + 8, :] for i in range(8)]
+    w = [img_ref[8 * i:8 * i + 8, :] for i in range(8)]
+    sub = lax.broadcasted_iota(jnp.int32, (8, 128), 0)
+    lane = lax.broadcasted_iota(jnp.int32, (8, K), 1)
+    row = lax.broadcasted_iota(jnp.int32, (8, K), 0)
+    for n in range(8):
+        col = [[jnp.broadcast_to(g[i][:, 8 * n + k:8 * n + k + 1], (8, 128)) for i in range(n, 8)] for k in range(8)]
+        at = {(h, k): jnp.broadcast_to(col[k][0][h:h + 1, :], (8, 128)) for k in range(8) for h in range(k + 1)}
+        scale = jnp.zeros((8, 128), F32)
+        for k in range(8):
+            inv = 1.0 / at[k, k]
+            scale = jnp.where(sub == k, at[k, k], scale)
+            m = [c * inv for c in col[k]]
+            m[0] = jnp.where(sub > k, m[0], 0.0)
+            for k2 in range(k + 1, 8):
+                f = at[k, k2] * inv
+                for k1 in range(k + 1, k2 + 1):
+                    at[k1, k2] = at[k1, k2] - at[k, k1] * f
+                for i in range(8 - n):
+                    col[k2][i] = col[k2][i] - m[i] * at[k, k2]
+            gp = jnp.broadcast_to(g[n][k:k + 1, :], (8, K))
+            wp = jnp.broadcast_to(w[n][k:k + 1, :], (8, ROWS))
+            for i in range(n, 8):
+                g[i] = g[i] - m[i - n][:, :K] * gp
+                w[i] = w[i] - jnp.concatenate([m[i - n], m[i - n]], axis=1) * wp
+        root = lax.rsqrt(scale)
+        r_ref[8 * n:8 * n + 8, :] = jnp.where(lane >= row + 8 * n, g[n] * root[:, :K], 0.0)
+        basis_ref[8 * n:8 * n + 8, :] = w[n] * jnp.concatenate([root, root], axis=1)
+
+
+def factor(gram, image):
+    return pl.pallas_call(
+        factor_kernel,
+        out_shape=(jax.ShapeDtypeStruct((K, ROWS), F32), jax.ShapeDtypeStruct((K, K), F32)),
+        name="cholesky_solve",
+    )(gram, image)
+
+
 def on_device(activations, start_basis):
-    image, gram = comm(activations, start_basis)
-    lower = jnp.linalg.cholesky(gram.reshape(K, K))
-    new_basis = jax.scipy.linalg.solve_triangular(lower, image.T, lower=True).T
-    return (new_basis, lower.T)
+    image, gram = comm(activations, start_basis.T)
+    basis, rfactor = factor(gram.reshape(K, K), image)
+    return (basis.T, rfactor)
 
 
 def solution(mesh):

time: 94 us -> 79.3 us (0.84)
  other arithmetic: 12.1 us -> 0 us
  local copies, waits for them, and re-layouts: 3.83 us -> 0 us
  Pallas kernels: 76.2 us -> 78.5 us
  matrix products: 0.95 us -> 0 us
    another operation x4 -> x0, other arithmetic: 11.4 us -> none  [the longest x3 6.52 us: on_device(): lower = jnp.linalg.cholesky(gram.reshape(K, K))]
    unnamed x4 -> x0, local copies, waits for them, and re-layouts: 3.76 us -> none
    pallas_call x1 -> x2, Pallas kernels: 76.2 us -> 78.5 us  [the longest x1 75.1 us: comm(): pl.pallas_call(comm_kernel, out_shape=(jax.ShapeDtypeStruct((K, ROWS), F3...]
    another operation x1 -> x0, matrix products: 0.95 us -> none  [on_device(): new_basis = jax.scipy.linalg.solve_triangular(lower, image.T, lower=True).T]
where the time goes in v2:
time: 79.3 us; the launch traced here: 79.1 us
  Pallas kernels  78.5 us (99%)
    pallas_call x1, Pallas kernels, comm(): pl.pallas_call(comm_kernel, out_shape=(jax.ShapeDtypeStruct((K, ROWS), F3...  75.1 us
    pallas_call x1, Pallas kernels, factor(): pl.pallas_call(factor_kernel, out_shape=(jax.ShapeDtypeStruct((K, ROWS),...  3.36 us

profile of v2, /device:TPU:1, one launch (start us, length us, event | category | flops | bytes accessed | tf_op | source)
XLA Modules:
  0.0 79.1 jit_solution(5295378201800644859)
XLA Ops:
  0.6 75.1 %reduce_project_gram.1 = (f32[64,256]{1,0:T(8,128)}, f32[32,2,64]{2,1,0:T(2,128)}) custom-call(bf16[256,8192]{1,0:T(8,128)(2,1)} %a_hbm.1, bf16[64,256]{1,0:T(8,128)(2,1)} %bitcast.3), custom_call_target="tpu_custom_call" | custom-call | flops 536870912 | bytes 4194304 | tf_op jit(solution)/shard_map/reduce_project_gram/pallas_call | solution.py:292
  75.7 3.4 %cholesky_solve.1 = (f32[64,256]{1,0:T(8,128)}, f32[64,64]{1,0:T(8,128)}) custom-call(f32[64,64]{1,0:T(8,128)} %bitcast.4, f32[64,256]{1,0:T(8,128)} %get-tuple-element.7.img_ref), custom_call_target="tpu_custom_call" | custom-call | tf_op jit(solution)/shard_map/cholesky_solve/pallas_call | solution.py:355

commit v3 on v2

--- a/solution.py
+++ b/solution.py
@@ -38,53 +38,40 @@
         return pltpu.make_async_remote_copy(src_ref=src, dst_ref=dst, send_sem=ss, recv_sem=rs, device_id=target,
                                             device_id_type=MESH)
 
+    me_a = (x, y)
+    me_b = (y, x)
+    steps = (2, 1, 3, 0)
+
+    def chunk(half, q, t):
+        return (c if half == 0 else 1 - c) * 8 + q * 4 + (me_a[q] + steps[t]) % 4
+
+    def load(half, q, t):
+        ch = chunk(half, q, t)
+        src = a_hbm.at[:, pl.ds(pl.multiple_of(ch * CHUNK, CHUNK), CHUNK)]
+        return pltpu.make_async_copy(src, a_v.at[ch], load_sem.at[(t * 2 + half) * 2 + q])
+
+    load_s = pltpu.make_async_copy(s_hbm, s_v, load_sem.at[16])
+    load_s.start()
+    for t in range(4):
+        for half in (1, 0):
+            for q in range(2):
+                load(half, q, t).start()
+
     bar = pltpu.get_barrier_semaphore()
-
-    @pl.loop(1, 16)
-    def _(k):
-        pl.semaphore_signal(bar, inc=1, device_id=dev(x, y, (z + 8 + k // 2 * (1 - k % 2 * 2) + 16) % 16, c), device_id_type=MESH)
-
-    @pl.loop(1, 32)
-    def _(k):
+    for k in (8, 7, 9, 6, 10, 5, 11, 4, 12, 3, 13, 2, 14, 1, 15):
+        pl.semaphore_signal(bar, inc=1, device_id=dev(x, y, (z + k) % 16, c), device_id_type=MESH)
+    for k in range(1, 32):
         xx, yy, cc = plane(k)
         pl.semaphore_signal(bar, inc=1, device_id=dev(xx, yy, z, cc), device_id_type=MESH)
 
-    pltpu.make_async_copy(s_hbm, s_v, load_sem.at[16]).start()
-    order = []
-    for half in (1, 0):
-        for j in range(8):
-            order.append((half, j))
-    for half, j in order:
-        ch = (c if half == 0 else 1 - c) * 8 + j
-        pltpu.make_async_copy(a_hbm.at[:, pl.ds(pl.multiple_of(ch * CHUNK, CHUNK), CHUNK)], a_v.at[ch], load_sem.at[ch]).start()
-
-    pltpu.make_async_copy(s_hbm, s_v, load_sem.at[16]).wait()
+    load_s.wait()
     st = s_v[...]
 
-    def partial(ch, j, dst):
-        pltpu.make_async_copy(a_hbm.at[:, pl.ds(0, CHUNK)], a_v.at[ch], load_sem.at[ch]).wait()
-        part = jnp.dot(st, a_v[ch], preferred_element_type=F32)
-        q, a = j // 4, j % 4
+    def partial(half, q, t, dst):
+        part = jnp.dot(st, a_v[chunk(half, q, t)], preferred_element_type=F32)
         for s in range(4):
             for b in range(4):
-                dst[q * 4 + s, a, b] = part[16 * s:16 * s + 16, 128 * b:128 * b + 128]
-
-    @pl.loop(0, 8)
-    def _(j):
-        partial((1 - c) * 8 + j, j, other)
-
-    pl.semaphore_wait(bar, 46)
-
-    c_copies = [remote(other.at[i], land_c.at[i], c_send.at[i], c_recv.at[i], partner) for i in range(8)]
-    for cp in c_copies:
-        cp.start()
-
-    @pl.loop(0, 8)
-    def _(j):
-        partial(c * 8 + j, j, r1)
-
-    me_a = (x, y)
-    me_b = (y, x)
+                dst[q * 4 + s, (me_a[q] + steps[t]) % 4, b] = part[16 * s:16 * s + 16, 128 * b:128 * b + 128]
 
     def first_peer(q, k):
         return dev((x + k) % 4, y, z, c) if q == 0 else dev(x, (y + k) % 4, z, c)
@@ -92,17 +79,43 @@
     def second_peer(q, k):
         return first_peer(1 - q, k)
 
+    def c_copy(q, t):
+        a = (me_a[q] + steps[t]) % 4
+        four = pl.ds(q * 4, 4)
+        return remote(other.at[four, a], land_c.at[four, a], c_send.at[t * 2 + q], c_recv.at[t * 2 + q], partner)
+
     copies_1 = {}
-    for s in range(4):
-        for q in range(2):
-            i = q * 4 + s
-            c_copies[i].wait_recv()
-            r1[i] = r1[i] + land_c[i]
-            for k in (1, 2, 3):
-                n = i * 3 + k - 1
-                cp = remote(r1.at[i, (me_a[q] + k) % 4], land_1.at[i, k - 1], s1_send.at[n], s1_recv.at[n], first_peer(q, k))
-                cp.start()
-                copies_1[i, k] = cp
+
+    def first_axis(t):
+        k = steps[t]
+        for q in range(2):
+            c_copy(q, t).wait_recv()
+            a = (me_a[q] + k) % 4
+            for s in range(4):
+                i = q * 4 + s
+                r1[i, a] = r1[i, a] + land_c[i, a]
+                if k:
+                    n = i * 3 + k - 1
+                    copies_1[i, k] = remote(r1.at[i, a], land_1.at[i, k - 1], s1_send.at[n], s1_recv.at[n], first_peer(q, k))
+                    copies_1[i, k].start()
+
+    for t in range(4):
+        for half in (1, 0):
+            for q in range(2):
+                load(half, q, t).wait()
+        for q in range(2):
+            partial(1, q, t, other)
+        if t == 0:
+            pl.semaphore_wait(bar, 46)
+        for q in range(2):
+            c_copy(q, t).start()
+        for q in range(2):
+            partial(0, q, t, r1)
+        if t >= 2:
+            first_axis(t - 2)
+    first_axis(2)
+    first_axis(3)
+
     copies_2 = {}
     for s in range(4):
         for q in range(2):
@@ -152,8 +165,7 @@
             total = total + land_z[k]
         pall[place(my_q), my_s] = (total * (1.0 / math.sqrt(TOTAL))).astype(BF16)
 
-        @pl.loop(1, 16)
-        def _(k):
+        for k in (8, 7, 9, 6, 10, 5, 11, 4, 12, 3, 13, 2, 14, 1, 15):
             zg_copy(k).start()
 
     def xy_copy(k, q, s):
@@ -170,8 +182,7 @@
             here = pall.at[place(q), s]
             pltpu.make_async_copy(here, here, zg_recv.at[q * 4 + s]).wait()
 
-        @pl.loop(1, 16)
-        def _(k, q=q, s=s):
+        for k in range(1, 16):
             xy_copy(k, q, s).start()
 
     def forward(k, q):
@@ -182,19 +193,18 @@
     for q in range(2):
         forward(0, q)[1].start()
 
-    @pl.loop(1, 16)
-    def _(k):
+    for k in range(1, 16):
         for q in range(2):
             p, cp = forward(k, q)
             pltpu.make_async_copy(pall.at[p], pall.at[p], xy_recv.at[k, q]).wait()
             cp.start()
 
     def image_part(half, acc):
-        def body(j, acc):
+        for j in range(8):
             ch = half * 8 + j
             pt = jnp.concatenate([pall[ch * 4 + b].reshape(64, 128) for b in range(4)], axis=1)
-            return acc + lax.dot_general(pt, a_v[ch], (((1,), (1,)), ((), ())), preferred_element_type=F32)
-        return lax.fori_loop(0, 8, body, acc)
+            acc = acc + lax.dot_general(pt, a_v[ch], (((1,), (1,)), ((), ())), preferred_element_type=F32)
+        return acc
 
     acc = image_part(c, jnp.zeros((K, ROWS), F32))
     theirs = pall.at[pl.ds((1 - c) * 32, 32)]
@@ -211,80 +221,59 @@
 
     def g1_copy(k):
         xx, yy, cc = plane(k)
-        return remote(g_own.at[(xx * 4 + yy) * 2 + cc], land_g.at[k], g1_send.at[k], g1_recv.at[k], dev(xx, yy, z, cc))
-
-    @pl.loop(1, 32)
-    def _(k):
+        return remote(g_own.at[(xx * 4 + yy) * 2 + cc], land_g.at[k], g1_send, g1_recv, dev(xx, yy, z, cc))
+
+    for k in range(1, 32):
         g1_copy(k).start()
 
-    tot = g_own[me]
-    for k in range(1, 32):
-        g1_copy(k).wait_recv()
-    for k in range(1, 32):
-        tot = tot + land_g[k]
-    g_z[z] = tot
-
-    def g2_copy(k, zs):
-        return remote(g_z.at[zs], g_z.at[zs], g2_send.at[k], g2_recv.at[zs], dev(x, y, (z + k) % 16, c))
-
-    @pl.loop(1, 16)
-    def _(k):
-        g2_copy(k, z).start()
-
-    @pl.loop(1, 16)
-    def _(k):
-        g2_copy(k, (z + k) % 16).wait_recv()
-
-    tot = g_z[0]
-    for k in range(1, 16):
-        tot = tot + g_z[k]
-    g_all[me] = tot
-
-    def g3_copy(k):
-        xx, yy, cc = plane(k)
-        return remote(g_all.at[me], g_all.at[me], g3_send.at[k], g3_recv.at[me], dev(xx, yy, z, cc))
-
-    @pl.loop(1, 32)
-    def _(k):
-        g3_copy(k).start()
-
-    @pl.loop(1, 32)
-    def _(k):
-        xx, yy, cc = plane(k)
-        m = (xx * 4 + yy) * 2 + cc
-        pltpu.make_async_copy(g_all.at[m], g_all.at[m], g3_recv.at[m]).wait()
-
-    gram_ref[...] = g_all[...]
-
-    for cp in c_copies:
-        cp.wait_send()
+    for t in range(4):
+        for q in range(2):
+            c_copy(q, t).wait_send()
     for i in range(8):
         for k in (1, 2, 3):
             copies_1[i, k].wait_send()
             copies_2[i, k].wait_send()
-    for i in range(8):
+
         @pl.when(4 * (i % 4) + 2 * (i // 4) + c != z)
         def _(i=i):
             z_copy(i, 1)[1].wait_send()
 
     @pl.when(owner)
     def _():
-        @pl.loop(1, 16)
-        def _(k):
+        for k in range(1, 16):
             zg_copy(k).wait_send()
 
-    @pl.loop(1, 16)
-    def _(k):
+    for k in range(1, 16):
         for q in range(2):
             pltpu.make_async_copy(pall.at[q], pall.at[q], xy_send.at[k, q]).wait()
+    pltpu.make_async_copy(theirs, theirs, f_send).wait()
+
+    most = land_g.at[pl.ds(1, 31)]
+    pltpu.make_async_copy(most, most, g1_recv).wait()
+    g_z[z] = g_own[me] + jnp.sum(land_g[1:32], axis=0)
+
+    def g2_copy(k, zs):
+        return remote(g_z.at[zs], g_z.at[zs], g2_send.at[k], g2_recv.at[zs], dev(x, y, (z + k) % 16, c))
+
+    for k in (8, 7, 9, 6, 10, 5, 11, 4, 12, 3, 13, 2, 14, 1, 15):
+        g2_copy(k, z).start()
+    pltpu.make_async_copy(most, most, g1_send).wait()
+    for k in range(1, 16):
+        g2_copy(k, (z + k) % 16).wait_recv()
+    g_all[me] = jnp.sum(g_z[...], axis=0)
+
+    def g3_copy(k):
+        xx, yy, cc = plane(k)
+        return remote(g_all.at[me], g_all.at[me], g3_send, g3_recv, dev(xx, yy, z, cc))
+
+    for k in range(1, 32):
+        g3_copy(k).start()
+    for k in range(1, 16):
         g2_copy(k, z).wait_send()
-
-    pltpu.make_async_copy(theirs, theirs, f_send).wait()
-
-    @pl.loop(1, 32)
-    def _(k):
-        g1_copy(k).wait_send()
-        g3_copy(k).wait_send()
+    others = g_all.at[pl.ds(0, 31)]
+    pltpu.make_async_copy(others, others, g3_recv).wait()
+    gram_ref[...] = g_all[...]
+    pltpu.make_async_copy(others, others, g3_send).wait()
 
 
 def comm(activations, start_basis):
@@ -312,7 +301,7 @@
             pltpu.VMEM((32, 2, K), F32),
             dma((17,)), dma((8,)), dma((8,)), dma((24,)), dma((24,)), dma((24,)), dma((24,)), dma((8,)), dma((16,)),
             dma((16,)), dma((8,)), dma((16, 2)), dma((16, 2)), dma, dma,
-            dma((32,)), dma((32,)), dma((16,)), dma((16,)), dma((32,)), dma((32,)),
+            dma, dma, dma((16,)), dma((16,)), dma, dma,
         ],
         compiler_params=pltpu.CompilerParams(collective_id=0, has_side_effects=True, vmem_limit_bytes=60 << 20),
         cost_estimate=pl.CostEstimate(flops=4 * ROWS * D * K, bytes_accessed=ROWS * D * 2, transcendentals=0),

time: 79.3 us -> 75.6 us (0.953)
  Pallas kernels: 78.5 us -> 74.7 us
    pallas_call x1, Pallas kernels: 75.1 us -> 71.4 us  [comm(): pl.pallas_call(comm_kernel, out_shape=(jax.ShapeDtypeStruct((K, ROWS), F3...]
where the time goes in v3:
time: 75.6 us; the launch traced here: 75.4 us
  Pallas kernels  74.7 us (99%)
    pallas_call x1, Pallas kernels, comm(): pl.pallas_call(comm_kernel, out_shape=(jax.ShapeDtypeStruct((K, ROWS), F3...  71.4 us
    pallas_call x1, Pallas kernels, factor(): pl.pallas_call(factor_kernel, out_shape=(jax.ShapeDtypeStruct((K, ROWS),...  3.36 us

profile of v3, /device:TPU:1, one launch (start us, length us, event | category | flops | bytes accessed | tf_op | source)
XLA Modules:
  0.0 75.4 jit_solution(4123099613359683173)
XLA Ops:
  0.6 71.4 %reduce_project_gram.1 = (f32[64,256]{1,0:T(8,128)}, f32[32,2,64]{2,1,0:T(2,128)}) custom-call(bf16[256,8192]{1,0:T(8,128)(2,1)} %a_hbm.1, bf16[64,256]{1,0:T(8,128)(2,1)} %bitcast.3), custom_call_target="tpu_custom_call" | custom-call | flops 536870912 | bytes 4194304 | tf_op jit(solution)/shard_map/reduce_project_gram/pallas_call | solution.py:281
  72.0 3.4 %cholesky_solve.1 = (f32[64,256]{1,0:T(8,128)}, f32[64,64]{1,0:T(8,128)}) custom-call(f32[64,64]{1,0:T(8,128)} %bitcast.4, f32[64,256]{1,0:T(8,128)} %get-tuple-element.7.img_ref), custom_call_target="tpu_custom_call" | custom-call | tf_op jit(solution)/shard_map/cholesky_solve/pallas_call | solution.py:344

commit v4 on v3

--- a/solution.py
+++ b/solution.py
@@ -20,7 +20,7 @@
                 g_own, land_g, g_z, g_all,
                 load_sem, c_send, c_recv, s1_send, s1_recv, s2_send, s2_recv, z_send, z_recv,
                 zg_send, zg_recv, xy_send, xy_recv, f_send, f_recv,
-                g1_send, g1_recv, g2_send, g2_recv, g3_send, g3_recv):
+                g1_send, g1_recv, g2_send, g2_recv, g3_send, g3_recv, know):
     r = lax.axis_index("rows")
     g = lax.axis_index("grp")
     x, z = r // 16, r % 16
@@ -49,6 +49,19 @@
         ch = chunk(half, q, t)
         src = a_hbm.at[:, pl.ds(pl.multiple_of(ch * CHUNK, CHUNK), CHUNK)]
         return pltpu.make_async_copy(src, a_v.at[ch], load_sem.at[(t * 2 + half) * 2 + q])
+
+    bar = pltpu.get_barrier_semaphore()
+    x_peers = [dev((x + k) % 4, y, z, c) for k in (1, 2, 3)]
+    y_peers = [dev(x, (y + k) % 4, z, c) for k in (1, 2, 3)]
+
+    def z_peers(k):
+        return [dev(x, y, (z + k) % 16, c), dev(x, y, (z + 16 - k) % 16, c)]
+
+    def greet(sem, targets):
+        for target in targets:
+            pl.semaphore_signal(sem, inc=1, device_id=target, device_id_type=MESH)
+
+    greet(bar, [partner] + x_peers + y_peers + z_peers(1))
 
     load_s = pltpu.make_async_copy(s_hbm, s_v, load_sem.at[16])
     load_s.start()
@@ -56,13 +69,6 @@
         for half in (1, 0):
             for q in range(2):
                 load(half, q, t).start()
-
-    bar = pltpu.get_barrier_semaphore()
-    for k in (8, 7, 9, 6, 10, 5, 11, 4, 12, 3, 13, 2, 14, 1, 15):
-        pl.semaphore_signal(bar, inc=1, device_id=dev(x, y, (z + k) % 16, c), device_id_type=MESH)
-    for k in range(1, 32):
-        xx, yy, cc = plane(k)
-        pl.semaphore_signal(bar, inc=1, device_id=dev(xx, yy, z, cc), device_id_type=MESH)
 
     load_s.wait()
     st = s_v[...]
@@ -106,15 +112,22 @@
         for q in range(2):
             partial(1, q, t, other)
         if t == 0:
-            pl.semaphore_wait(bar, 46)
+            pl.semaphore_wait(bar, 9)
         for q in range(2):
             c_copy(q, t).start()
+        if t == 0:
+            greet(know.at[0], y_peers)
+            greet(know.at[1], z_peers(1))
         for q in range(2):
             partial(0, q, t, r1)
         if t >= 2:
             first_axis(t - 2)
     first_axis(2)
     first_axis(3)
+    pl.semaphore_wait(know.at[0], 3)
+    greet(know.at[2], [partner])
+    pl.semaphore_wait(know.at[1], 2)
+    greet(know.at[3], z_peers(2))
 
     copies_2 = {}
     for s in range(4):
@@ -129,6 +142,9 @@
                 cp.start()
                 copies_2[i, k] = cp
 
+    pl.semaphore_wait(know.at[3], 2)
+    greet(know.at[4], z_peers(4))
+
     def z_copy(i, slot):
         zo = 4 * (i % 4) + 2 * (i // 4) + c
         return zo, remote(r3.at[i], land_z.at[slot], z_send.at[i], z_recv.at[slot], dev(x, y, zo, c))
@@ -139,6 +155,8 @@
             for k in (1, 2, 3):
                 copies_2[i, k].wait_recv()
             r3[i] = (r2[i, me_b[q]] + land_2[i, 0]) + (land_2[i, 1] + land_2[i, 2])
+            if i == 0:
+                pl.semaphore_wait(know.at[4], 2)
             zo = 4 * s + 2 * q + c
 
             @pl.when(zo != z)
@@ -223,6 +241,7 @@
         xx, yy, cc = plane(k)
         return remote(g_own.at[(xx * 4 + yy) * 2 + cc], land_g.at[k], g1_send, g1_recv, dev(xx, yy, z, cc))
 
+    pl.semaphore_wait(know.at[2], 1)
     for k in range(1, 32):
         g1_copy(k).start()
 
@@ -301,7 +320,7 @@
             pltpu.VMEM((32, 2, K), F32),
             dma((17,)), dma((8,)), dma((8,)), dma((24,)), dma((24,)), dma((24,)), dma((24,)), dma((8,)), dma((16,)),
             dma((16,)), dma((8,)), dma((16, 2)), dma((16, 2)), dma, dma,
-            dma, dma, dma((16,)), dma((16,)), dma, dma,
+            dma, dma, dma((16,)), dma((16,)), dma, dma, pltpu.SemaphoreType.REGULAR((5,)),
         ],
         compiler_params=pltpu.CompilerParams(collective_id=0, has_side_effects=True, vmem_limit_bytes=60 << 20),
         cost_estimate=pl.CostEstimate(flops=4 * ROWS * D * K, bytes_accessed=ROWS * D * 2, transcendentals=0),

time: 75.6 us -> 73.2 us (0.968)
  Pallas kernels: 74.7 us -> 72.4 us
    pallas_call x1, Pallas kernels: 71.4 us -> 69.1 us  [comm(): pl.pallas_call(comm_kernel, out_shape=(jax.ShapeDtypeStruct((K, ROWS), F3...]
where the time goes in v4:
time: 73.2 us; the launch traced here: 73.1 us
  Pallas kernels  72.4 us (99%)
    pallas_call x1, Pallas kernels, comm(): pl.pallas_call(comm_kernel, out_shape=(jax.ShapeDtypeStruct((K, ROWS), F3...  69.1 us
    pallas_call x1, Pallas kernels, factor(): pl.pallas_call(factor_kernel, out_shape=(jax.ShapeDtypeStruct((K, ROWS),...  3.36 us

profile of v4, /device:TPU:1, one launch (start us, length us, event | category | flops | bytes accessed | tf_op | source)
XLA Modules:
  0.0 73.1 jit_solution(5057982665608740363)
XLA Ops:
  0.6 69.1 %reduce_project_gram.1 = (f32[64,256]{1,0:T(8,128)}, f32[32,2,64]{2,1,0:T(2,128)}) custom-call(bf16[256,8192]{1,0:T(8,128)(2,1)} %a_hbm.1, bf16[64,256]{1,0:T(8,128)(2,1)} %bitcast.3), custom_call_target="tpu_custom_call" | custom-call | flops 536870912 | bytes 4194304 | tf_op jit(solution)/shard_map/reduce_project_gram/pallas_call | solution.py:300
  69.7 3.4 %cholesky_solve.1 = (f32[64,256]{1,0:T(8,128)}, f32[64,64]{1,0:T(8,128)}) custom-call(f32[64,64]{1,0:T(8,128)} %bitcast.4, f32[64,256]{1,0:T(8,128)} %get-tuple-element.7.img_ref), custom_call_target="tpu_custom_call" | custom-call | tf_op jit(solution)/shard_map/cholesky_solve/pallas_call | solution.py:363

commit v5 on v4

--- a/solution.py
+++ b/solution.py
@@ -38,6 +38,9 @@
         return pltpu.make_async_remote_copy(src_ref=src, dst_ref=dst, send_sem=ss, recv_sem=rs, device_id=target,
                                             device_id_type=MESH)
 
+    def arrived(ref, sem):
+        pltpu.make_async_copy(ref, ref, sem).wait()
+
     me_a = (x, y)
     me_b = (y, x)
     steps = (2, 1, 3, 0)
@@ -48,7 +51,7 @@
     def load(half, q, t):
         ch = chunk(half, q, t)
         src = a_hbm.at[:, pl.ds(pl.multiple_of(ch * CHUNK, CHUNK), CHUNK)]
-        return pltpu.make_async_copy(src, a_v.at[ch], load_sem.at[(t * 2 + half) * 2 + q])
+        return pltpu.make_async_copy(src, a_v.at[ch], load_sem.at[t])
 
     bar = pltpu.get_barrier_semaphore()
     x_peers = [dev((x + k) % 4, y, z, c) for k in (1, 2, 3)]
@@ -63,7 +66,7 @@
 
     greet(bar, [partner] + x_peers + y_peers + z_peers(1))
 
-    load_s = pltpu.make_async_copy(s_hbm, s_v, load_sem.at[16])
+    load_s = pltpu.make_async_copy(s_hbm, s_v, load_sem.at[4])
     load_s.start()
     for t in range(4):
         for half in (1, 0):
@@ -88,29 +91,25 @@
     def c_copy(q, t):
         a = (me_a[q] + steps[t]) % 4
         four = pl.ds(q * 4, 4)
-        return remote(other.at[four, a], land_c.at[four, a], c_send.at[t * 2 + q], c_recv.at[t * 2 + q], partner)
-
-    copies_1 = {}
+        return remote(other.at[four, a], land_c.at[four, a], c_send, c_recv.at[t], partner)
 
     def first_axis(t):
         k = steps[t]
-        for q in range(2):
-            c_copy(q, t).wait_recv()
+        arrived(land_c.at[pl.ds(0, 2)], c_recv.at[t])
+        for q in range(2):
             a = (me_a[q] + k) % 4
             for s in range(4):
                 i = q * 4 + s
                 r1[i, a] = r1[i, a] + land_c[i, a]
                 if k:
-                    n = i * 3 + k - 1
-                    copies_1[i, k] = remote(r1.at[i, a], land_1.at[i, k - 1], s1_send.at[n], s1_recv.at[n], first_peer(q, k))
-                    copies_1[i, k].start()
+                    remote(r1.at[i, a], land_1.at[i, k - 1], s1_send, s1_recv.at[s], first_peer(q, k)).start()
 
     for t in range(4):
-        for half in (1, 0):
-            for q in range(2):
-                load(half, q, t).wait()
+        arrived(a_v.at[pl.ds(0, 4)], load_sem.at[t])
         for q in range(2):
             partial(1, q, t, other)
+        for q in range(2):
+            partial(0, q, t, r1)
         if t == 0:
             pl.semaphore_wait(bar, 9)
         for q in range(2):
@@ -118,42 +117,32 @@
         if t == 0:
             greet(know.at[0], y_peers)
             greet(know.at[1], z_peers(1))
-        for q in range(2):
-            partial(0, q, t, r1)
-        if t >= 2:
-            first_axis(t - 2)
-    first_axis(2)
+        if t >= 1:
+            first_axis(t - 1)
     first_axis(3)
     pl.semaphore_wait(know.at[0], 3)
     greet(know.at[2], [partner])
     pl.semaphore_wait(know.at[1], 2)
     greet(know.at[3], z_peers(2))
-
-    copies_2 = {}
+    pl.semaphore_wait(know.at[3], 2)
+    greet(know.at[4], z_peers(4))
+
     for s in range(4):
+        arrived(land_1.at[pl.ds(0, 2)], s1_recv.at[s])
         for q in range(2):
             i = q * 4 + s
-            for k in (1, 2, 3):
-                copies_1[i, k].wait_recv()
             r2[i] = (r1[i, me_a[q]] + land_1[i, 0]) + (land_1[i, 1] + land_1[i, 2])
             for k in (1, 2, 3):
-                n = i * 3 + k - 1
-                cp = remote(r2.at[i, (me_b[q] + k) % 4], land_2.at[i, k - 1], s2_send.at[n], s2_recv.at[n], second_peer(q, k))
-                cp.start()
-                copies_2[i, k] = cp
-
-    pl.semaphore_wait(know.at[3], 2)
-    greet(know.at[4], z_peers(4))
+                remote(r2.at[i, (me_b[q] + k) % 4], land_2.at[i, k - 1], s2_send, s2_recv.at[s], second_peer(q, k)).start()
 
     def z_copy(i, slot):
         zo = 4 * (i % 4) + 2 * (i // 4) + c
-        return zo, remote(r3.at[i], land_z.at[slot], z_send.at[i], z_recv.at[slot], dev(x, y, zo, c))
+        return zo, remote(r3.at[i], land_z.at[slot], z_send, z_recv, dev(x, y, zo, c))
 
     for s in range(4):
+        arrived(land_2.at[pl.ds(0, 2)], s2_recv.at[s])
         for q in range(2):
             i = q * 4 + s
-            for k in (1, 2, 3):
-                copies_2[i, k].wait_recv()
             r3[i] = (r2[i, me_b[q]] + land_2[i, 0]) + (land_2[i, 1] + land_2[i, 2])
             if i == 0:
                 pl.semaphore_wait(know.at[4], 2)
@@ -172,13 +161,12 @@
 
     def zg_copy(k):
         here = pall.at[place(my_q), my_s]
-        return remote(here, here, zg_send.at[k], zg_recv.at[my_i], dev(x, y, (z + k) % 16, c))
+        return remote(here, here, zg_send, zg_recv.at[my_i], dev(x, y, (z + k) % 16, c))
 
     @pl.when(owner)
     def _():
         total = r3[my_i]
-        for k in range(1, 16):
-            pltpu.make_async_copy(land_z.at[k], land_z.at[k], z_recv.at[k]).wait()
+        arrived(land_z.at[pl.ds(1, 15)], z_recv)
         for k in range(1, 16):
             total = total + land_z[k]
         pall[place(my_q), my_s] = (total * (1.0 / math.sqrt(TOTAL))).astype(BF16)
@@ -186,9 +174,12 @@
         for k in (8, 7, 9, 6, 10, 5, 11, 4, 12, 3, 13, 2, 14, 1, 15):
             zg_copy(k).start()
 
+    def far(k):
+        return min(k // 4, 4 - k // 4) + min(k % 4, 4 - k % 4)
+
     def xy_copy(k, q, s):
         here = pall.at[place(q), s]
-        return remote(here, here, xy_send.at[k, q], xy_recv.at[k, q], dev((x + k // 4) % 4, (y + k % 4) % 4, z, c))
+        return remote(here, here, xy_send, xy_recv.at[far(k) - 1], dev((x + k // 4) % 4, (y + k % 4) % 4, z, c))
 
     for j in range(8):
         off = jnp.where(owner, (0, 2, 14, 4, 12, 6, 10, 8)[j], (1, 15, 3, 13, 5, 11, 7, 9)[j])
@@ -197,8 +188,7 @@
 
         @pl.when(off != 0)
         def _(s=s, q=q):
-            here = pall.at[place(q), s]
-            pltpu.make_async_copy(here, here, zg_recv.at[q * 4 + s]).wait()
+            arrived(pall.at[place(q), s], zg_recv.at[q * 4 + s])
 
         for k in range(1, 16):
             xy_copy(k, q, s).start()
@@ -206,16 +196,17 @@
     def forward(k, q):
         xx, yy = (x - k // 4 + 4) % 4, (y - k % 4 + 4) % 4
         p = (c * 2 + q) * 16 + (xx * 4 + yy if q == 0 else yy * 4 + xx)
-        return p, remote(pall.at[p], pall.at[p], f_send, f_recv, partner)
+        return remote(pall.at[p], pall.at[p], f_send, f_recv, partner)
 
     for q in range(2):
-        forward(0, q)[1].start()
-
-    for k in range(1, 16):
-        for q in range(2):
-            p, cp = forward(k, q)
-            pltpu.make_async_copy(pall.at[p], pall.at[p], xy_recv.at[k, q]).wait()
-            cp.start()
+        forward(0, q).start()
+
+    for hops in range(1, 5):
+        ring = [k for k in range(1, 16) if far(k) == hops]
+        arrived(pall.at[pl.ds(0, 2 * len(ring))], xy_recv.at[hops - 1])
+        for k in ring:
+            for q in range(2):
+                forward(k, q).start()
 
     def image_part(half, acc):
         for j in range(8):
@@ -226,7 +217,7 @@
 
     acc = image_part(c, jnp.zeros((K, ROWS), F32))
     theirs = pall.at[pl.ds((1 - c) * 32, 32)]
-    pltpu.make_async_copy(theirs, theirs, f_recv).wait()
+    arrived(theirs, f_recv)
     acc = image_part(1 - c, acc)
     img = acc * (1.0 / math.sqrt(D))
     img_ref[...] = img
@@ -245,40 +236,34 @@
     for k in range(1, 32):
         g1_copy(k).start()
 
-    for t in range(4):
-        for q in range(2):
-            c_copy(q, t).wait_send()
-    for i in range(8):
-        for k in (1, 2, 3):
-            copies_1[i, k].wait_send()
-            copies_2[i, k].wait_send()
-
-        @pl.when(4 * (i % 4) + 2 * (i // 4) + c != z)
-        def _(i=i):
-            z_copy(i, 1)[1].wait_send()
+    arrived(other, c_send)
+    arrived(r1.at[pl.ds(0, 6)], s1_send)
+    arrived(r2.at[pl.ds(0, 6)], s2_send)
 
     @pl.when(owner)
     def _():
-        for k in range(1, 16):
-            zg_copy(k).wait_send()
-
-    for k in range(1, 16):
-        for q in range(2):
-            pltpu.make_async_copy(pall.at[q], pall.at[q], xy_send.at[k, q]).wait()
-    pltpu.make_async_copy(theirs, theirs, f_send).wait()
+        arrived(r3.at[pl.ds(0, 7)], z_send)
+        arrived(land_z.at[pl.ds(0, 15), pl.ds(0, 8)], zg_send)
+
+    @pl.when(jnp.logical_not(owner))
+    def _():
+        arrived(r3, z_send)
+
+    arrived(pall.at[pl.ds(0, 30)], xy_send)
+    arrived(theirs, f_send)
 
     most = land_g.at[pl.ds(1, 31)]
-    pltpu.make_async_copy(most, most, g1_recv).wait()
+    arrived(most, g1_recv)
     g_z[z] = g_own[me] + jnp.sum(land_g[1:32], axis=0)
 
-    def g2_copy(k, zs):
-        return remote(g_z.at[zs], g_z.at[zs], g2_send.at[k], g2_recv.at[zs], dev(x, y, (z + k) % 16, c))
+    def g2_copy(k):
+        return remote(g_z.at[z], g_z.at[z], g2_send, g2_recv, dev(x, y, (z + k) % 16, c))
 
     for k in (8, 7, 9, 6, 10, 5, 11, 4, 12, 3, 13, 2, 14, 1, 15):
-        g2_copy(k, z).start()
-    pltpu.make_async_copy(most, most, g1_send).wait()
-    for k in range(1, 16):
-        g2_copy(k, (z + k) % 16).wait_recv()
+        g2_copy(k).start()
+    arrived(most, g1_send)
+    line = g_z.at[pl.ds(0, 15)]
+    arrived(line, g2_recv)
     g_all[me] = jnp.sum(g_z[...], axis=0)
 
     def g3_copy(k):
@@ -287,12 +272,11 @@
 
     for k in range(1, 32):
         g3_copy(k).start()
-    for k in range(1, 16):
-        g2_copy(k, z).wait_send()
+    arrived(line, g2_send)
     others = g_all.at[pl.ds(0, 31)]
-    pltpu.make_async_copy(others, others, g3_recv).wait()
+    arrived(others, g3_recv)
     gram_ref[...] = g_all[...]
-    pltpu.make_async_copy(others, others, g3_send).wait()
+    arrived(others, g3_send)
 
 
 def comm(activations, start_basis):
@@ -318,9 +302,9 @@
             pltpu.VMEM((32, 2, K), F32),
             pltpu.VMEM((16, 2, K), F32),
             pltpu.VMEM((32, 2, K), F32),
-            dma((17,)), dma((8,)), dma((8,)), dma((24,)), dma((24,)), dma((24,)), dma((24,)), dma((8,)), dma((16,)),
-            dma((16,)), dma((8,)), dma((16, 2)), dma((16, 2)), dma, dma,
-            dma, dma, dma((16,)), dma((16,)), dma, dma, pltpu.SemaphoreType.REGULAR((5,)),
+            dma((5,)), dma, dma((4,)), dma, dma((4,)), dma, dma((4,)), dma, dma,
+            dma, dma((8,)), dma, dma((4,)), dma, dma,
+            dma, dma, dma, dma, dma, dma, pltpu.SemaphoreType.REGULAR((5,)),
         ],
         compiler_params=pltpu.CompilerParams(collective_id=0, has_side_effects=True, vmem_limit_bytes=60 << 20),
         cost_estimate=pl.CostEstimate(flops=4 * ROWS * D * K, bytes_accessed=ROWS * D * 2, transcendentals=0),

time: 73.2 us -> 69.5 us (0.949)
  Pallas kernels: 72.4 us -> 68.7 us
    pallas_call x1, Pallas kernels: 69.1 us -> 65.3 us  [comm(): pl.pallas_call(comm_kernel, out_shape=(jax.ShapeDtypeStruct((K, ROWS), F3...]
where the time goes in v5:
time: 69.5 us; the launch traced here: 69.3 us
  Pallas kernels  68.7 us (99%)
    pallas_call x1, Pallas kernels, comm(): pl.pallas_call(comm_kernel, out_shape=(jax.ShapeDtypeStruct((K, ROWS), F3...  65.3 us
    pallas_call x1, Pallas kernels, factor(): pl.pallas_call(factor_kernel, out_shape=(jax.ShapeDtypeStruct((K, ROWS),...  3.36 us

profile of v5, /device:TPU:1, one launch (start us, length us, event | category | flops | bytes accessed | tf_op | source)
XLA Modules:
  0.0 69.3 jit_solution(4650557856664042603)
XLA Ops:
  0.6 65.3 %reduce_project_gram.1 = (f32[64,256]{1,0:T(8,128)}, f32[32,2,64]{2,1,0:T(2,128)}) custom-call(bf16[256,8192]{1,0:T(8,128)(2,1)} %a_hbm.1, bf16[64,256]{1,0:T(8,128)(2,1)} %bitcast.3), custom_call_target="tpu_custom_call" | custom-call | flops 536870912 | bytes 4194304 | tf_op jit(solution)/shard_map/reduce_project_gram/pallas_call | solution.py:284
  66.0 3.4 %cholesky_solve.1 = (f32[64,256]{1,0:T(8,128)}, f32[64,64]{1,0:T(8,128)}) custom-call(f32[64,64]{1,0:T(8,128)} %bitcast.4, f32[64,256]{1,0:T(8,128)} %get-tuple-element.7.img_ref), custom_call_target="tpu_custom_call" | custom-call | tf_op jit(solution)/shard_map/cholesky_solve/pallas_call | solution.py:347

commit v6 on v5

--- a/solution.py
+++ b/solution.py
@@ -13,6 +13,7 @@
 BF16 = jnp.bfloat16
 ROWS, D, K = 256, 8192, 64
 TOTAL = 131072
+OWNERS = ((3, 13, 8, 9, 5, 7, 11, 10), (14, 6, 8, 9, 4, 12, 11, 10))
 CHUNK = 512
 
 
@@ -135,9 +136,11 @@
             for k in (1, 2, 3):
                 remote(r2.at[i, (me_b[q] + k) % 4], land_2.at[i, k - 1], s2_send, s2_recv.at[s], second_peer(q, k)).start()
 
+    owners = [jnp.where(c == 0, OWNERS[0][i], OWNERS[1][i]) for i in range(8)]
+
     def z_copy(i, slot):
-        zo = 4 * (i % 4) + 2 * (i // 4) + c
-        return zo, remote(r3.at[i], land_z.at[slot], z_send, z_recv, dev(x, y, zo, c))
+        zo = owners[i]
+        return remote(r3.at[i], land_z.at[slot], z_send, z_recv, dev(x, y, zo, c))
 
     for s in range(4):
         arrived(land_2.at[pl.ds(0, 2)], s2_recv.at[s])
@@ -146,15 +149,15 @@
             r3[i] = (r2[i, me_b[q]] + land_2[i, 0]) + (land_2[i, 1] + land_2[i, 2])
             if i == 0:
                 pl.semaphore_wait(know.at[4], 2)
-            zo = 4 * s + 2 * q + c
+            zo = owners[i]
 
             @pl.when(zo != z)
             def _(i=i, zo=zo):
-                z_copy(i, (zo - z + 16) % 16)[1].start()
-
-    my_s, my_q = z // 4, (z % 4) // 2
-    my_i = my_q * 4 + my_s
-    owner = z % 2 == c
+                z_copy(i, (zo - z + 16) % 16).start()
+
+    my_i = sum(jnp.where(owners[i] == z, i, 0) for i in range(8))
+    my_s, my_q = my_i % 4, my_i // 4
+    owner = sum(jnp.where(owners[i] == z, 1, 0) for i in range(8)) == 1
 
     def place(q):
         return (c * 2 + q) * 16 + jnp.where(q == 0, x * 4 + y, y * 4 + x)
@@ -181,12 +184,10 @@
         here = pall.at[place(q), s]
         return remote(here, here, xy_send, xy_recv.at[far(k) - 1], dev((x + k // 4) % 4, (y + k % 4) % 4, z, c))
 
-    for j in range(8):
-        off = jnp.where(owner, (0, 2, 14, 4, 12, 6, 10, 8)[j], (1, 15, 3, 13, 5, 11, 7, 9)[j])
-        zz = (z + off) % 16
-        s, q = zz // 4, (zz % 4) // 2
-
-        @pl.when(off != 0)
+    for i in (6, 7, 3, 2, 1, 5, 4, 0):
+        q, s = i // 4, i % 4
+
+        @pl.when(z != owners[i])
         def _(s=s, q=q):
             arrived(pall.at[place(q), s], zg_recv.at[q * 4 + s])
 

time: 69.5 us -> 69.3 us (level)
  no operation moved by 1% of the time
where the time goes in v6:
time: 69.3 us; the launch traced here: 69.1 us
  Pallas kernels  68.5 us (99%)
    pallas_call x1, Pallas kernels, comm(): pl.pallas_call(comm_kernel, out_shape=(jax.ShapeDtypeStruct((K, ROWS), F3...  65.1 us
    pallas_call x1, Pallas kernels, factor(): pl.pallas_call(factor_kernel, out_shape=(jax.ShapeDtypeStruct((K, ROWS),...  3.36 us

profile of v6, /device:TPU:1, one launch (start us, length us, event | category | flops | bytes accessed | tf_op | source)
XLA Modules:
  0.0 69.1 jit_solution(7024276825409894424)
XLA Ops:
  0.6 65.1 %reduce_project_gram.1 = (f32[64,256]{1,0:T(8,128)}, f32[32,2,64]{2,1,0:T(2,128)}) custom-call(bf16[256,8192]{1,0:T(8,128)(2,1)} %a_hbm.1, bf16[64,256]{1,0:T(8,128)(2,1)} %bitcast.3), custom_call_target="tpu_custom_call" | custom-call | flops 536870912 | bytes 4194304 | tf_op jit(solution)/shard_map/reduce_project_gram/pallas_call | solution.py:285
  65.8 3.4 %cholesky_solve.1 = (f32[64,256]{1,0:T(8,128)}, f32[64,64]{1,0:T(8,128)}) custom-call(f32[64,64]{1,0:T(8,128)} %bitcast.4, f32[64,256]{1,0:T(8,128)} %get-tuple-element.7.img_ref), custom_call_target="tpu_custom_call" | custom-call | tf_op jit(solution)/shard_map/cholesky_solve/pallas_call | solution.py:348

commit v7 on v6

--- a/solution.py
+++ b/solution.py
@@ -17,7 +17,7 @@
 CHUNK = 512
 
 
-def comm_kernel(a_hbm, s_hbm, img_ref, gram_ref, a_v, s_v, other, land_c, r1, land_1, r2, land_2, r3, land_z, pall,
+def comm_kernel(a_hbm, s_hbm, img_ref, gram_ref, a_v, s_v, other, land_c, r1, out_1, land_1, r2, land_2, r3, land_z, pall,
                 g_own, land_g, g_z, g_all,
                 load_sem, c_send, c_recv, s1_send, s1_recv, s2_send, s2_recv, z_send, z_recv,
                 zg_send, zg_recv, xy_send, xy_recv, f_send, f_recv,
@@ -101,9 +101,12 @@
             a = (me_a[q] + k) % 4
             for s in range(4):
                 i = q * 4 + s
-                r1[i, a] = r1[i, a] + land_c[i, a]
-                if k:
-                    remote(r1.at[i, a], land_1.at[i, k - 1], s1_send, s1_recv.at[s], first_peer(q, k)).start()
+                part = r1[i, a] + land_c[i, a]
+                if k == 0:
+                    r1[i, a] = part
+                else:
+                    out_1[i, a] = part.astype(BF16)
+                    remote(out_1.at[i, a], land_1.at[i, k - 1], s1_send, s1_recv.at[s], first_peer(q, k)).start()
 
     for t in range(4):
         arrived(a_v.at[pl.ds(0, 4)], load_sem.at[t])
@@ -132,7 +135,7 @@
         arrived(land_1.at[pl.ds(0, 2)], s1_recv.at[s])
         for q in range(2):
             i = q * 4 + s
-            r2[i] = (r1[i, me_a[q]] + land_1[i, 0]) + (land_1[i, 1] + land_1[i, 2])
+            r2[i] = (r1[i, me_a[q]] + land_1[i, 0].astype(F32)) + (land_1[i, 1].astype(F32) + land_1[i, 2].astype(F32))
             for k in (1, 2, 3):
                 remote(r2.at[i, (me_b[q] + k) % 4], land_2.at[i, k - 1], s2_send, s2_recv.at[s], second_peer(q, k)).start()
 
@@ -238,7 +241,7 @@
         g1_copy(k).start()
 
     arrived(other, c_send)
-    arrived(r1.at[pl.ds(0, 6)], s1_send)
+    arrived(out_1.at[pl.ds(0, 6)], s1_send)
     arrived(r2.at[pl.ds(0, 6)], s2_send)
 
     @pl.when(owner)
@@ -293,7 +296,8 @@
             pltpu.VMEM((8, 4, 4, 16, 128), F32),
             pltpu.VMEM((8, 4, 4, 16, 128), F32),
             pltpu.VMEM((8, 4, 4, 16, 128), F32),
-            pltpu.VMEM((8, 3, 4, 16, 128), F32),
+            pltpu.VMEM((8, 4, 4, 16, 128), BF16),
+            pltpu.VMEM((8, 3, 4, 16, 128), BF16),
             pltpu.VMEM((8, 4, 16, 128), F32),
             pltpu.VMEM((8, 3, 16, 128), F32),
             pltpu.VMEM((8, 16, 128), F32),

time: 69.3 us -> 66.9 us (0.965)
  Pallas kernels: 68.5 us -> 66.1 us
    pallas_call x1, Pallas kernels: 65.1 us -> 62.7 us  [comm(): pl.pallas_call(comm_kernel, out_shape=(jax.ShapeDtypeStruct((K, ROWS), F3...]
where the time goes in v7:
time: 66.9 us; the launch traced here: 66.7 us
  Pallas kernels  66.1 us (99%)
    pallas_call x1, Pallas kernels, comm(): pl.pallas_call(comm_kernel, out_shape=(jax.ShapeDtypeStruct((K, ROWS), F3...  62.7 us
    pallas_call x1, Pallas kernels, factor(): pl.pallas_call(factor_kernel, out_shape=(jax.ShapeDtypeStruct((K, ROWS),...  3.36 us

profile of v7, /device:TPU:1, one launch (start us, length us, event | category | flops | bytes accessed | tf_op | source)
XLA Modules:
  0.0 66.7 jit_solution(3475450954919848486)
XLA Ops:
  0.6 62.7 %reduce_project_gram.1 = (f32[64,256]{1,0:T(8,128)}, f32[32,2,64]{2,1,0:T(2,128)}) custom-call(bf16[256,8192]{1,0:T(8,128)(2,1)} %a_hbm.1, bf16[64,256]{1,0:T(8,128)(2,1)} %bitcast.3), custom_call_target="tpu_custom_call" | custom-call | flops 536870912 | bytes 4194304 | tf_op jit(solution)/shard_map/reduce_project_gram/pallas_call | solution.py:288
  63.3 3.4 %cholesky_solve.1 = (f32[64,256]{1,0:T(8,128)}, f32[64,64]{1,0:T(8,128)}) custom-call(f32[64,64]{1,0:T(8,128)} %bitcast.4, f32[64,256]{1,0:T(8,128)} %get-tuple-element.7.img_ref), custom_call_target="tpu_custom_call" | custom-call | tf_op jit(solution)/shard_map/cholesky_solve/pallas_call | solution.py:352

commit v8 on v7

--- a/solution.py
+++ b/solution.py
@@ -228,13 +228,14 @@
     gram = lax.dot_general(img, img, (((1,), (1,)), ((), ())), precision=lax.Precision.HIGHEST, preferred_element_type=F32)
     gram = gram * (1.0 / TOTAL)
 
-    for m in range(32):
-        g_own[m] = gram[2 * m:2 * m + 2, :]
-    me = (x * 4 + y) * 2 + c
+    for m in range(8):
+        g_own[m] = jnp.concatenate([gram[8 * m:8 * m + 4, :], gram[8 * m + 4:8 * m + 8, :]], axis=1)
+    me = y * 2 + c
+    seat = x * 8 + me
 
     def g1_copy(k):
         xx, yy, cc = plane(k)
-        return remote(g_own.at[(xx * 4 + yy) * 2 + cc], land_g.at[k], g1_send, g1_recv, dev(xx, yy, z, cc))
+        return remote(g_own.at[yy * 2 + cc], land_g.at[seat], g1_send, g1_recv, dev(xx, yy, z, cc))
 
     pl.semaphore_wait(know.at[2], 1)
     for k in range(1, 32):
@@ -256,9 +257,10 @@
     arrived(pall.at[pl.ds(0, 30)], xy_send)
     arrived(theirs, f_send)
 
-    most = land_g.at[pl.ds(1, 31)]
+    land_g[seat] = g_own[me]
+    most = land_g.at[pl.ds(0, 31)]
     arrived(most, g1_recv)
-    g_z[z] = g_own[me] + jnp.sum(land_g[1:32], axis=0)
+    g_z[z] = jnp.sum(land_g[...], axis=0)
 
     def g2_copy(k):
         return remote(g_z.at[z], g_z.at[z], g2_send, g2_recv, dev(x, y, (z + k) % 16, c))
@@ -274,10 +276,10 @@
         xx, yy, cc = plane(k)
         return remote(g_all.at[me], g_all.at[me], g3_send, g3_recv, dev(xx, yy, z, cc))
 
-    for k in range(1, 32):
+    for k in range(1, 8):
         g3_copy(k).start()
     arrived(line, g2_send)
-    others = g_all.at[pl.ds(0, 31)]
+    others = g_all.at[pl.ds(0, 7)]
     arrived(others, g3_recv)
     gram_ref[...] = g_all[...]
     arrived(others, g3_send)
@@ -287,7 +289,7 @@
     dma = pltpu.SemaphoreType.DMA
     return pl.pallas_call(
         comm_kernel,
-        out_shape=(jax.ShapeDtypeStruct((K, ROWS), F32), jax.ShapeDtypeStruct((32, 2, K), F32)),
+        out_shape=(jax.ShapeDtypeStruct((K, ROWS), F32), jax.ShapeDtypeStruct((8, 4, 128), F32)),
         in_specs=[pl.BlockSpec(memory_space=pl.ANY)] * 2,
         out_specs=(pl.BlockSpec(memory_space=pltpu.VMEM),) * 2,
         scratch_shapes=[
@@ -303,10 +305,10 @@
             pltpu.VMEM((8, 16, 128), F32),
             pltpu.VMEM((16, 16, 128), F32),
             pltpu.VMEM((64, 4, 16, 128), BF16),
-            pltpu.VMEM((32, 2, K), F32),
-            pltpu.VMEM((32, 2, K), F32),
-            pltpu.VMEM((16, 2, K), F32),
-            pltpu.VMEM((32, 2, K), F32),
+            pltpu.VMEM((8, 4, 128), F32),
+            pltpu.VMEM((32, 4, 128), F32),
+            pltpu.VMEM((16, 4, 128), F32),
+            pltpu.VMEM((8, 4, 128), F32),
             dma((5,)), dma, dma((4,)), dma, dma((4,)), dma, dma((4,)), dma, dma,
             dma, dma((8,)), dma, dma((4,)), dma, dma,
             dma, dma, dma, dma, dma, dma, pltpu.SemaphoreType.REGULAR((5,)),
@@ -318,7 +320,7 @@
 
 
 def factor_kernel(gram_ref, img_ref, basis_ref, r_ref):
-    g = [gram_ref[8 * i:8 * i + 8, :] for i in range(8)]
+    g = [jnp.concatenate([gram_ref[i][:, :K], gram_ref[i][:, K:]], axis=0) for i in range(8)]
     w = [img_ref[8 * i:8 * i + 8, :] for i in range(8)]
     sub = lax.broadcasted_iota(jnp.int32, (8, 128), 0)
     lane = lax.broadcasted_iota(jnp.int32, (8, K), 1)
@@ -358,7 +360,7 @@
 
 def on_device(activations, start_basis):
     image, gram = comm(activations, start_basis.T)
-    basis, rfactor = factor(gram.reshape(K, K), image)
+    basis, rfactor = factor(gram, image)
     return (basis.T, rfactor)
 
 

time: 66.9 us -> 66.3 us (level)
    pallas_call x1, Pallas kernels: 62.7 us -> 62 us  [comm(): pl.pallas_call(comm_kernel, out_shape=(jax.ShapeDtypeStruct((K, ROWS), F3...]
where the time goes in v8:
time: 66.3 us; the launch traced here: 66.1 us
  Pallas kernels  65.5 us (99%)
    pallas_call x1, Pallas kernels, comm(): pl.pallas_call(comm_kernel, out_shape=(jax.ShapeDtypeStruct((K, ROWS), F3...  62 us
    pallas_call x1, Pallas kernels, factor(): pl.pallas_call(factor_kernel, out_shape=(jax.ShapeDtypeStruct((K, ROWS),...  3.45 us

profile of v8, /device:TPU:1, one launch (start us, length us, event | category | flops | bytes accessed | tf_op | source)
XLA Modules:
  0.0 66.1 jit_solution(16112008331072649595)
XLA Ops:
  0.6 62.0 %reduce_project_gram.1 = (f32[64,256]{1,0:T(8,128)}, f32[8,4,128]{2,1,0:T(4,128)}) custom-call(bf16[256,8192]{1,0:T(8,128)(2,1)} %a_hbm.1, bf16[64,256]{1,0:T(8,128)(2,1)} %bitcast.2), custom_call_target="tpu_custom_call" | custom-call | flops 536870912 | bytes 4194304 | tf_op jit(solution)/shard_map/reduce_project_gram/pallas_call | solution.py:290
  62.7 3.4 %cholesky_solve.1 = (f32[64,256]{1,0:T(8,128)}, f32[64,64]{1,0:T(8,128)}) custom-call(f32[8,4,128]{2,1,0:T(4,128)} %get-tuple-element.6.gram_ref, f32[64,256]{1,0:T(8,128)} %get-tuple-element.7.img_ref), custom_call_target="tpu_custom_call" | custom-call | tf_op jit(solution)/shard_map/cholesky_solve/pallas_call | solution.py:354

commit v9 on v8

--- a/solution.py
+++ b/solution.py
@@ -123,11 +123,12 @@
             greet(know.at[1], z_peers(1))
         if t >= 1:
             first_axis(t - 1)
+        if t == 3:
+            pl.semaphore_wait(know.at[0], 3)
+            greet(know.at[2], [partner])
+            pl.semaphore_wait(know.at[1], 2)
+            greet(know.at[3], z_peers(2))
     first_axis(3)
-    pl.semaphore_wait(know.at[0], 3)
-    greet(know.at[2], [partner])
-    pl.semaphore_wait(know.at[1], 2)
-    greet(know.at[3], z_peers(2))
     pl.semaphore_wait(know.at[3], 2)
     greet(know.at[4], z_peers(4))
 

time: 66.3 us -> 66.3 us (level)
  no operation moved by 1% of the time
where the time goes in v9:
time: 66.3 us; the launch traced here: 66.1 us
  Pallas kernels  65.4 us (99%)
    pallas_call x1, Pallas kernels, comm(): pl.pallas_call(comm_kernel, out_shape=(jax.ShapeDtypeStruct((K, ROWS), F3...  62 us
    pallas_call x1, Pallas kernels, factor(): pl.pallas_call(factor_kernel, out_shape=(jax.ShapeDtypeStruct((K, ROWS),...  3.45 us

profile of v9, /device:TPU:1, one launch (start us, length us, event | category | flops | bytes accessed | tf_op | source)
XLA Modules:
  0.0 66.1 jit_solution(13865931206974825349)
XLA Ops:
  0.6 62.0 %reduce_project_gram.1 = (f32[64,256]{1,0:T(8,128)}, f32[8,4,128]{2,1,0:T(4,128)}) custom-call(bf16[256,8192]{1,0:T(8,128)(2,1)} %a_hbm.1, bf16[64,256]{1,0:T(8,128)(2,1)} %bitcast.2), custom_call_target="tpu_custom_call" | custom-call | flops 536870912 | bytes 4194304 | tf_op jit(solution)/shard_map/reduce_project_gram/pallas_call | solution.py:291
  62.6 3.4 %cholesky_solve.1 = (f32[64,256]{1,0:T(8,128)}, f32[64,64]{1,0:T(8,128)}) custom-call(f32[8,4,128]{2,1,0:T(4,128)} %get-tuple-element.6.gram_ref, f32[64,256]{1,0:T(8,128)} %get-tuple-element.7.img_ref), custom_call_target="tpu_custom_call" | custom-call | tf_op jit(solution)/shard_map/cholesky_solve/pallas_call | solution.py:355
